TPU v7x, 32 devices: a whole 2x2x4 slice. The times are simulated.
32 devices in a mesh: dp: 4 (over y, core), row: 2 (over x), col: 4 (over z).
Axes of the slice: x: 2, y: 2, z: 4, core: 2. Of those that a mesh axis runs over, the one named last changes fastest.
Arguments:
- tokens: bfloat16 [1024, 6144], P(('dp', 'col'), 'row'), may hold values from -6 to 6
- cotangent: bfloat16 [1024, 6144], P(('dp', 'col'), 'row'), may hold values from -6 to 6
- pre_act: bfloat16 [1024, 12288], P('dp', 'col'), may hold values from -6 to 6
- weight_in: bfloat16 [6144, 12288], P('row', 'col'), may hold values from -0.078125 to 0.078125
- weight_out: bfloat16 [12288, 6144], P('col', 'row'), may hold values from -0.0546875 to 0.0546875
Outputs:
- grad_tokens: bfloat16 [1024, 6144], P(('dp', 'col'), 'row')
- grad_in: float32 [6144, 12288], P('row', ('col', 'dp'))
- grad_out: float32 [12288, 6144], P(('col', 'dp'), 'row')
All inputs are finite; a program needn't handle non-finite values.
Results may differ from a plain program's by a relative error of at most 0.023.
Values may be sent and summed in bfloat16 or wider, within the bound.
A program may use at most 192 MiB of HBM per device.

v0:
```python
import jax
import jax.numpy as jnp
from jax import lax
from jax.sharding import PartitionSpec as P


def gelu_value(a):
    return 0.5 * a * (1.0 + lax.erf(a * 0.7071067811865476))


def gelu_slope(a):
    return (
        0.5 * (1.0 + lax.erf(a * 0.7071067811865476))
        + a * jnp.exp(-0.5 * a * a) * 0.3989422804014327
    )


def shards(tokens, cotangent, pre_act, weight_in, weight_out):
    contract = (((1,), (1,)), ((), ()))
    lead = (((0,), (0,)), ((), ()))
    tok_all, cot_all = (
        lax.all_gather(tokens, "col", axis=0, tiled=True),
        lax.all_gather(cotangent, "col", axis=0, tiled=True),
    )
    replica = tok_all.shape[0]
    total_tokens = replica * lax.axis_size("dp")
    factor = float(total_tokens) ** (-0.5)
    pre_float = pre_act.astype(jnp.float32)
    summed = lax.psum(
        lax.dot_general(cot_all, weight_out, contract, preferred_element_type=jnp.float32).astype(
            jnp.bfloat16
        ),
        "row",
    ).astype(jnp.float32)
    grad_pre = (summed * gelu_slope(pre_float)).astype(jnp.bfloat16)
    grad_tokens = lax.psum_scatter(
        lax.dot_general(grad_pre, weight_in, contract, preferred_element_type=jnp.float32).astype(
            jnp.bfloat16
        ),
        "col",
        scatter_dimension=0,
        tiled=True,
    )
    hidden = gelu_value(pre_float).astype(jnp.bfloat16)
    first = lax.dot_general(tok_all, grad_pre, lead, preferred_element_type=jnp.float32) * factor
    second = lax.dot_general(hidden, cot_all, lead, preferred_element_type=jnp.float32) * factor
    grad_in, grad_out = (
        lax.psum_scatter(first.astype(jnp.bfloat16), "dp", scatter_dimension=1, tiled=True).astype(
            jnp.float32
        ),
        lax.psum_scatter(second.astype(jnp.bfloat16), "dp", scatter_dimension=0, tiled=True).astype(
            jnp.float32
        ),
    )
    return (grad_tokens, grad_in, grad_out)


def solution(mesh):
    in_specs = (
        P(("dp", "col"), "row"),
        P(("dp", "col"), "row"),
        P("dp", "col"),
        P("row", "col"),
        P("col", "row"),
    )
    out_specs = (P(("dp", "col"), "row"), P("row", ("col", "dp")), P(("col", "dp"), "row"))
    return jax.shard_map(shards, mesh=mesh, in_specs=in_specs, out_specs=out_specs, check_vma=False)
```

profile of v0, /device:TPU:0, one launch (start us, length us, event | category | flops | bytes accessed | tf_op | source)
XLA Modules:
  0.0 469.2 jit_solution(8932405080684482068)
XLA Ops:
  7.2 0.0 all-gather.3.cloned.1.call-start
  7.2 0.7 all-gather.3.cloned.1.call-update
  7.9 0.0 all-gather.5.cloned.1.call-start
  7.9 0.7 all-gather.5.cloned.1.call-update
  8.6 0.0 copy-start
  8.7 0.0 all-reduce.2.cloned.1.call-start
  8.7 40.7 %all-gather.3.cloned.1.call-done = bf16[256,3072]{1,0:T(8,128)(2,1)} async-done(((bf16[64,3072]{1,0:T(8,128)(2,1)}), bf16[256,3072]{1,0:T(8,128)(2,1)}) %all-gather.3.cloned.1.call-update) | async-done | bytes 1572880 | tf_op jit(solution)/shard_map/all_gather | solution.py:23
  49.4 0.0 copy-start.2
  49.4 12.7 %convolution_convert_fusion.1 = bf16[256,3072]{1,0:T(8,128)(2,1)} fusion(bf16[256,3072]{1,0:T(8,128)(2,1)} %all-gather.3.cloned.1.call-done, bf16[3072,3072]{1,0:T(8,128)(2,1)} %param.9), kind=kOutput, calls=%fused_computation.9 | convolution fusion | flops 4832624640 | bytes 22020096 | tf_op jit(solution)/shard_map/dot_general | solution.py:30
  62.1 0.0 all-reduce.2.cloned.1.call-update
  62.1 0.0 reduce-scatter.8.cloned.1.call-start
  62.1 0.0 copy-done
  62.1 0.0 copy-done.2
  62.2 9.3 %multiply_convert_fusion = bf16[3072,3072]{1,0:T(8,128)(2,1)} fusion(bf16[256,3072]{1,0:T(8,128)(2,1)S(1)} %copy-done.2, bf16[256,3072]{1,0:T(8,128)(2,1)S(1)} %copy-done), kind=kOutput, calls=%fused_computation | convolution fusion | flops 4855431168 | bytes 22020096 | tf_op jit(solution)/shard_map/dot_general | solution.py:46
  71.5 0.0 reduce-scatter.8.cloned.1.call-update
  71.5 0.0 reduce-scatter.6.cloned.1.call-start
  71.5 15.4 %all-gather.5.cloned.1.call-done = bf16[256,3072]{1,0:T(8,128)(2,1)} async-done(((bf16[64,3072]{1,0:T(8,128)(2,1)}), bf16[256,3072]{1,0:T(8,128)(2,1)}) %all-gather.5.cloned.1.call-update) | async-done | bytes 1572880 | tf_op jit(solution)/shard_map/all_gather | solution.py:22
  86.9 53.3 %all-reduce.2.cloned.1.call-done = bf16[256,3072]{1,0:T(8,128)(2,1)} async-done(((bf16[256,3072]{1,0:T(8,128)(2,1)}), bf16[256,3072]{1,0:T(8,128)(2,1)}) %all-reduce.2.cloned.1.call-update) | async-done | bytes 1572880 | tf_op jit(solution)/shard_map/psum | solution.py:29
  140.2 13.6 %fusion = bf16[3072,3072]{0,1:T(8,128)(2,1)} fusion(bf16[256,3072]{1,0:T(8,128)(2,1)} %all-gather.5.cloned.1.call-done, bf16[256,3072]{1,0:T(8,128)(2,1)S(1)} %copy-done, bf16[256,3072]{1,0:T(8,128)(2,1)} %all-reduce.2.cloned.1.call-done), kind=kOutput, calls=%fused_computation.2 | convolution fusion | flops 4860149760 | bytes 23592960 | tf_op jit(solution)/shard_map/dot_general | solution.py:45
  153.8 0.0 copy-start.1
  153.8 0.0 reduce-scatter.6.cloned.1.call-update
  153.8 0.0 reduce-scatter.4.cloned.1.call-start
  153.9 1.8 copy-done.1
  155.7 14.6 %convolution_convert_fusion = bf16[256,3072]{1,0:T(8,128)(2,1)} fusion(bf16[3072,3072]{1,0:T(8,128)(2,1)} %param.8, bf16[256,3072]{1,0:T(8,128)(2,1)S(1)} %copy-done, bf16[256,3072]{1,0:T(8,128)(2,1)S(1)} %copy-done.1), kind=kOutput, calls=%fused_computation.8 | convolution fusion | flops 4842061824 | bytes 23592960 | tf_op jit(solution)/shard_map/dot_general | solution.py:37
  170.3 0.0 reduce-scatter.4.cloned.1.call-update
  170.3 112.0 %reduce-scatter.8.cloned.1.call-done = bf16[768,3072]{1,0:T(8,128)(2,1)} async-done(((bf16[3072,3072]{1,0:T(8,128)(2,1)}), bf16[768,3072]{1,0:T(8,128)(2,1)}) %reduce-scatter.8.cloned.1.call-update) | async-done | bytes 4718608 | tf_op jit(solution)/shard_map/reduce_scatter | solution.py:51
  282.2 7.4 %convert_element_type.43 = f32[768,3072]{1,0:T(8,128)} convert(bf16[768,3072]{1,0:T(8,128)(2,1)} %reduce-scatter.8.cloned.1.call-done) | non-fusion elementwise | flops 2359296 | bytes 14155776 | tf_op jit(solution)/shard_map/convert_element_type | solution.py:51
  289.6 134.6 %reduce-scatter.6.cloned.1.call-done = bf16[3072,768]{0,1:T(8,128)(2,1)} async-done(((bf16[3072,3072]{0,1:T(8,128)(2,1)}), bf16[3072,768]{0,1:T(8,128)(2,1)}) %reduce-scatter.6.cloned.1.call-update) | async-done | bytes 4718608 | tf_op jit(solution)/shard_map/reduce_scatter | solution.py:48
  424.2 7.4 %copy.8 = f32[3072,768]{1,0:T(8,128)} copy(bf16[3072,768]{0,1:T(8,128)(2,1)} %reduce-scatter.6.cloned.1.call-done) | data formatting | bytes 14155776
  431.6 30.8 %reduce-scatter.4.cloned.1.call-done = bf16[64,3072]{1,0:T(8,128)(2,1)} async-done(((bf16[256,3072]{1,0:T(8,128)(2,1)}), bf16[64,3072]{1,0:T(8,128)(2,1)}) %reduce-scatter.4.cloned.1.call-update) | async-done | bytes 393232 | tf_op jit(solution)/shard_map/reduce_scatter | solution.py:36
Async XLA Ops:
  7.2 42.2 %all-gather.3.cloned.1.call-start = ((), (), s32[]{:S(2)}) async-start(), calls=%async_computation.3 | async-start | bytes 1966080 | tf_op jit(solution)/shard_map/all_gather | solution.py:23
  7.9 79.1 %all-gather.5.cloned.1.call-start = ((), (), s32[]{:S(2)}) async-start(), calls=%async_computation.6 | async-start | bytes 1966080 | tf_op jit(solution)/shard_map/all_gather | solution.py:22
  8.6 53.5 %copy-start = (bf16[256,3072]{1,0:T(8,128)(2,1)S(1)}, bf16[256,3072]{1,0:T(8,128)(2,1)}, u32[]{:S(2)}) copy-start(bf16[256,3072]{1,0:T(8,128)(2,1)} %param.7) | copy-start | bytes 4718596
  8.7 131.5 %all-reduce.2.cloned.1.call-start = ((), (), s32[]{:S(2)}) async-start(), calls=%async_computation.4 | async-start | bytes 3145728 | tf_op jit(solution)/shard_map/psum | solution.py:29
  49.4 12.8 %copy-start.2 = (bf16[256,3072]{1,0:T(8,128)(2,1)S(1)}, bf16[256,3072]{1,0:T(8,128)(2,1)}, u32[]{:S(2)}) copy-start(bf16[256,3072]{1,0:T(8,128)(2,1)} %all-gather.3.cloned.1.call-done) | copy-start | bytes 4718596
  62.1 220.2 %reduce-scatter.8.cloned.1.call-start = ((), (), s32[]{:S(2)}) async-start(), calls=%async_computation.8 | async-start | bytes 23592960 | tf_op jit(solution)/shard_map/reduce_scatter | solution.py:51
  71.5 352.7 %reduce-scatter.6.cloned.1.call-start = ((), (), s32[]{:S(2)}) async-start(), calls=%async_computation.7 | async-start | bytes 23592960 | tf_op jit(solution)/shard_map/reduce_scatter | solution.py:48
  153.8 1.9 copy-start.1
  153.8 308.5 %reduce-scatter.4.cloned.1.call-start = ((), (), s32[]{:S(2)}) async-start(), calls=%async_computation.5 | async-start | bytes 1966080 | tf_op jit(solution)/shard_map/reduce_scatter | solution.py:36
Sparse Core Ops, SparseCore 0:
  9.6 39.7 all-gather.2
  51.0 35.9 all-gather.4
  89.8 50.3 all-reduce.1
  142.8 139.3 reduce-scatter.7
  284.7 139.4 reduce-scatter.5
  427.0 35.2 reduce-scatter.3
where the time goes:
time: 470 us; the launch traced here: 469 us
  waiting for transfers between devices  388 us (83%)
  matrix products  50.2 us (11%)
  between operations  14.1 us (3%)
  local copies, waits for them, and re-layouts  9.18 us (2%)
  other arithmetic  7.37 us (2%)
    reduce_scatter x1, waiting for transfers between devices, shards(): lax.psum_scatter(first.astype(jnp.bfloat16), 'dp', scatter_dimension=1, t...  135 us
    reduce_scatter x1, waiting for transfers between devices, shards(): lax.psum_scatter(second.astype(jnp.bfloat16), 'dp', scatter_dimension=0,...  112 us
    psum x1, waiting for transfers between devices, shards(): lax.psum(lax.dot_general(cot_all, weight_out, contract, preferred_element...  53.3 us
    all_gather x1, waiting for transfers between devices, shards(): lax.all_gather(cotangent, 'col', axis=0, tiled=True)  40.7 us
    reduce_scatter x1, waiting for transfers between devices, shards(): lax.psum_scatter(lax.dot_general(grad_pre, weight_in, contract, preferred...  30.8 us
    all_gather x1, waiting for transfers between devices, shards(): lax.all_gather(tokens, 'col', axis=0, tiled=True)  15.4 us
    dot_general x1, matrix products, shards(): lax.dot_general(grad_pre, weight_in, contract, preferred_element_type=jnp...  14.6 us
    dot_general x1, matrix products, shards(): lax.dot_general(tok_all, grad_pre, lead, preferred_element_type=jnp.float32)  13.6 us
  transfers between devices with their start and end apart: 6, of which 6 were waited for; matrix products, arithmetic and copies ran while one was open for 14% of the time, Pallas kernels for 0%

commit v1 on v0

v1 whole, which is shorter than its diff:
```python
import functools

import jax
import jax.numpy as jnp
from jax import lax
from jax.experimental import pallas as pl
from jax.experimental.pallas import tpu as pltpu
from jax.sharding import PartitionSpec as P

MESH = pl.DeviceIdType.MESH
NT = (((1,), (1,)), ((), ()))
TN = (((0,), (0,)), ((), ()))


def gelu_parts(a):
    half = 0.5 * (1.0 + lax.erf(a * 0.7071067811865476))
    return half * a, half + a * jnp.exp(-0.5 * a * a) * 0.3989422804014327


def tile_of(extent):
    return 256 if extent % 256 == 0 else 128


def body(
    n_dp, n_row, n_col,
    tok, cot, pre, w_in, w_out,
    tok_all, cot_all, gp_all, hid_all, grad_tok,
    win, wout, hid, slope, part, xrecv, gp, acc, cotg, term, rs,
    w_sem, l_sem, cz_s, cz_r, tz_s, tz_r, y_s, y_r, c_s, c_r,
    h_s, h_r, g_s, g_r, x_s, x_r, rs_s, rs_r,
):
    p, r, z = lax.axis_index("dp"), lax.axis_index("row"), lax.axis_index("col")
    n_y = n_dp // 2
    tokc, width = tok.shape
    rows = n_col * tokc
    hidden = pre.shape[1]
    hc = hidden // n_dp
    partner = p + 1 - 2 * lax.rem(p, 2)

    def dp_off(k):
        return lax.rem(p + k, n_dp)

    def remote(src, dst, send, recv, where):
        return pltpu.make_async_remote_copy(
            src_ref=src, dst_ref=dst, send_sem=send, recv_sem=recv,
            device_id=where, device_id_type=MESH,
        )

    wo = pltpu.make_async_copy(w_out, wout, w_sem.at[0])
    wi = pltpu.make_async_copy(w_in, win, w_sem.at[1])
    own = pltpu.make_async_copy(cot, cotg.at[z], l_sem.at[0])
    wo.start()
    own.start()

    barrier = pltpu.get_barrier_semaphore()
    for axis, me, count in (("dp", p, n_dp), ("row", r, n_row), ("col", z, n_col)):
        for k in range(1, count):
            pl.semaphore_signal(
                barrier, inc=1, device_id={axis: lax.rem(me + k, count)}, device_id_type=MESH
            )
    pl.semaphore_wait(barrier, n_dp + n_row + n_col - 3)

    sends = ((cotg, cot_all, cz_s, cz_r), (tok_all.at[p], tok_all, tz_s, tz_r))

    def z_copy(t, d, s, first):
        group, _, ss, rr = sends[t]
        blk = z - s if d == 0 else z + s
        src = (cot, tok)[t] if first else group.at[blk]
        to = z + 1 if d == 0 else z - 1
        return remote(src, group.at[blk], ss.at[d, s], rr.at[d, s + 1], {"col": to})

    def can_send(d, s):
        return (z - s >= 0) & (z + 1 < n_col) if d == 0 else (z + s < n_col) & (z - 1 >= 0)

    def has(d, s):
        return z - s >= 0 if d == 0 else z + s < n_col

    def y_send(t, src, blk):
        for k in range(1, n_y):
            remote(
                src, sends[t][1].at[p, blk], y_s.at[t, k], y_r.at[t, k], {"dp": dp_off(2 * k)}
            ).start()

    def z_start(t):
        for d in (0, 1):
            @pl.when(can_send(d, 0))
            def _():
                z_copy(t, d, 0, True).start()

    def z_step(t, s):
        for d in (0, 1):
            @pl.when(has(d, s))
            def _():
                blk = z - s if d == 0 else z + s
                group = sends[t][0]
                remote(
                    group.at[blk], group.at[blk], sends[t][2].at[d, s], sends[t][3].at[d, s],
                    {"col": lax.rem(z + 1, n_col)},
                ).wait_recv()
                if s < n_col - 1:
                    @pl.when(can_send(d, s))
                    def _():
                        z_copy(t, d, s, False).start()
                y_send(t, group.at[blk], blk)

    def whole(t, at, send, recv, who):
        return remote(
            sends[t][1].at[at], sends[t][1].at[at], send, recv, {"dp": who}
        )

    z_start(0)
    own_tok = pltpu.make_async_copy(tok, tok_all.at[p, z], l_sem.at[1])
    own_tok.start()
    y_send(0, cot, z)
    y_send(1, tok, z)
    wi.start()

    def gelu_chunk(i):
        step = 32
        def one(j, _):
            at = pl.ds(pl.multiple_of(j * step, step), step)
            a = pre[at, i * hc:(i + 1) * hc].astype(jnp.float32)
            value, sl = gelu_parts(a)
            hid[i, at, :] = value.astype(jnp.bfloat16)
            slope[i, at, :] = sl
            return 0
        lax.fori_loop(0, rows // step, one, 0)

    done = 0
    for s in range(1, n_col):
        upto = (n_dp * s + n_col - 2) // (n_col - 1)
        for i in range(done, upto):
            gelu_chunk(i)
        done = upto
        z_step(0, s)
        if s == min(2, n_col - 1):
            own_tok.wait()
            z_start(1)
    for k in range(1, n_dp):
        q = dp_off(k)
        remote(hid.at[q], hid_all.at[p], h_s.at[k], h_r.at[k], {"dp": q}).start()
    own_hid = pltpu.make_async_copy(hid.at[p], hid_all.at[p], l_sem.at[2])
    own_hid.start()

    own.wait()
    own_cot = pltpu.make_async_copy(cotg, cot_all.at[p], l_sem.at[0])
    own_cot.start()
    remote(cotg, cot_all.at[p], c_s.at[0, 0], c_r.at[0, 0], {"dp": partner}).start()
    wo.wait()

    ht = tile_of(hc)
    for i in range(n_dp):
        def ptile(j, _):
            off = pl.multiple_of(j * ht, ht)
            w = wout[pl.ds(i * hc + off, ht), :]
            lhs = cotg[...].reshape(rows, width)
            out = lax.dot_general(lhs, w, NT, preferred_element_type=jnp.float32)
            part[i, :, pl.ds(off, ht)] = out.astype(jnp.bfloat16)
            return 0
        lax.fori_loop(0, hc // ht, ptile, 0)
        for k in range(1, n_row):
            remote(
                part.at[i], xrecv.at[k - 1, i], x_s.at[k - 1, i], x_r.at[k - 1, i],
                {"row": lax.rem(r + k, n_row)},
            ).start()
    wi.wait()

    tok_steps = 1
    wt = tile_of(width)
    for i in range(n_dp):
        for k in range(1, n_row):
            remote(
                part.at[i], xrecv.at[k - 1, i], x_s.at[k - 1, i], x_r.at[k - 1, i],
                {"row": lax.rem(r + k, n_row)},
            ).wait_recv()
        step = 32
        def one(j, _):
            at = pl.ds(pl.multiple_of(j * step, step), step)
            total = part[i, at, :].astype(jnp.float32)
            for k in range(1, n_row):
                total = total + xrecv[k - 1, i, at, :].astype(jnp.float32)
            gp[i, at, :] = (total * slope[i, at, :]).astype(jnp.bfloat16)
            return 0
        lax.fori_loop(0, rows // step, one, 0)

        @pl.when(p == i)
        def _():
            pltpu.make_async_copy(gp.at[i], gp_all.at[p], l_sem.at[3]).start()

        @pl.when(p != i)
        def _():
            k = lax.rem(i - p + n_dp, n_dp)
            remote(gp.at[i], gp_all.at[p], g_s.at[k], g_r.at[k], {"dp": i}).start()

        def wtile(j, _):
            at = pl.ds(pl.multiple_of(j * wt, wt), wt)
            w = win[at, i * hc:(i + 1) * hc]
            out = lax.dot_general(gp[i], w, NT, preferred_element_type=jnp.float32)
            if i > 0:
                out = acc[:, at] + out
            if i < n_dp - 1:
                acc[:, at] = out
            else:
                term[:, :, at] = out.astype(jnp.bfloat16).reshape(n_col, tokc, wt)
            return 0
        lax.fori_loop(0, width // wt, wtile, 0)
        upto = ((n_col - 1) * (i + 1)) // n_dp
        while tok_steps <= upto:
            z_step(1, tok_steps)
            tok_steps += 1

    for k in range(1, n_col):
        to = lax.rem(z + k, n_col)
        remote(term.at[to], rs.at[k], rs_s.at[k], rs_r.at[k], {"col": to}).start()
    remote(tok_all.at[p], tok_all.at[p], c_s.at[1, 0], c_r.at[1, 0], {"dp": partner}).start()

    for t in (0, 1):
        for k in range(1, n_y):
            q = dp_off(n_dp - 2 * k)
            whole(t, q, y_s.at[t, k], y_r.at[t, k], q).wait_recv()
            whole(t, q, c_s.at[t, k], c_r.at[t, k], partner).start()

    for k in range(1, n_col):
        remote(term.at[z], rs.at[k], rs_s.at[k], rs_r.at[k], {"col": lax.rem(z + k, n_col)}).wait_recv()
    total = term[z].astype(jnp.float32)
    for k in range(1, n_col):
        total = total + rs[k].astype(jnp.float32)
    grad_tok[...] = total.astype(jnp.bfloat16)

    own_hid.wait()
    own_cot.wait()
    pltpu.make_async_copy(gp.at[p], gp_all.at[p], l_sem.at[3]).wait()
    for t in (0, 1):
        for d in (0, 1):
            for s in range(n_col - 1):
                @pl.when(can_send(d, s))
                def _():
                    z_copy(t, d, s, s == 0).wait_send()
        for k in range(1, n_y):
            whole(t, p, y_s.at[t, k], y_r.at[t, k], dp_off(2 * k)).wait_send()
        for k in range(n_y):
            q = dp_off(n_dp - 2 * k) if k else p
            whole(t, q, c_s.at[t, k], c_r.at[t, k], partner).wait()
    for k in range(1, n_dp):
        q = dp_off(k)
        remote(hid.at[q], hid_all.at[p], h_s.at[k], h_r.at[k], {"dp": q}).wait()
        remote(gp.at[q], gp_all.at[p], g_s.at[k], g_r.at[k], {"dp": q}).wait()
    for i in range(n_dp):
        for k in range(1, n_row):
            remote(
                part.at[i], xrecv.at[k - 1, i], x_s.at[k - 1, i], x_r.at[k - 1, i],
                {"row": lax.rem(r + k, n_row)},
            ).wait_send()
    for k in range(1, n_col):
        to = lax.rem(z + k, n_col)
        remote(term.at[to], rs.at[k], rs_s.at[k], rs_r.at[k], {"col": to}).wait_send()


def shards(n_dp, n_row, n_col, tokens, cotangent, pre_act, weight_in, weight_out):
    tokc, width = tokens.shape
    rows, hidden = pre_act.shape
    hc = hidden // n_dp
    n_y = n_dp // 2
    bf, f32 = jnp.bfloat16, jnp.float32
    dma = pltpu.SemaphoreType.DMA
    anywhere = pl.BlockSpec(memory_space=pl.ANY)
    vmem = pl.BlockSpec(memory_space=pltpu.VMEM)
    tok_all, cot_all, gp_all, hid_all, grad_tokens = pl.pallas_call(
        functools.partial(body, n_dp, n_row, n_col),
        out_shape=(
            jax.ShapeDtypeStruct((n_dp, n_col, tokc, width), bf),
            jax.ShapeDtypeStruct((n_dp, n_col, tokc, width), bf),
            jax.ShapeDtypeStruct((n_dp, rows, hc), bf),
            jax.ShapeDtypeStruct((n_dp, rows, hc), bf),
            jax.ShapeDtypeStruct((tokc, width), bf),
        ),
        in_specs=[anywhere, anywhere, vmem, anywhere, anywhere],
        out_specs=(anywhere, anywhere, anywhere, anywhere, vmem),
        scratch_shapes=[
            pltpu.VMEM((width, hidden), bf),
            pltpu.VMEM((hidden, width), bf),
            pltpu.VMEM((n_dp, rows, hc), bf),
            pltpu.VMEM((n_dp, rows, hc), f32),
            pltpu.VMEM((n_dp, rows, hc), bf),
            pltpu.VMEM((max(n_row - 1, 1), n_dp, rows, hc), bf),
            pltpu.VMEM((n_dp, rows, hc), bf),
            pltpu.VMEM((rows, width), f32),
            pltpu.VMEM((n_col, tokc, width), bf),
            pltpu.VMEM((n_col, tokc, width), bf),
            pltpu.VMEM((n_col, tokc, width), bf),
            dma((2,)), dma((4,)),
            dma((2, n_col)), dma((2, n_col)), dma((2, n_col)), dma((2, n_col)),
            dma((2, n_y)), dma((2, n_y)), dma((2, n_y)), dma((2, n_y)),
            dma((n_dp,)), dma((n_dp,)), dma((n_dp,)), dma((n_dp,)),
            dma((max(n_row - 1, 1), n_dp)), dma((max(n_row - 1, 1), n_dp)),
            dma((n_col,)), dma((n_col,)),
        ],
        compiler_params=pltpu.CompilerParams(
            collective_id=0, has_side_effects=True, vmem_limit_bytes=62 * 1024 * 1024
        ),
    )(tokens, cotangent, pre_act, weight_in, weight_out)
    total = n_dp * rows
    factor = float(total) ** (-0.5)
    tok_all, cot_all = tok_all.reshape(total, width), cot_all.reshape(total, width)
    gp_all, hid_all = gp_all.reshape(total, hc), hid_all.reshape(total, hc)
    grad_in = lax.dot_general(tok_all, gp_all, TN, preferred_element_type=f32) * factor
    grad_out = lax.dot_general(hid_all, cot_all, TN, preferred_element_type=f32) * factor
    return grad_tokens, grad_in, grad_out


def solution(mesh):
    in_specs = (
        P(("dp", "col"), "row"),
        P(("dp", "col"), "row"),
        P("dp", "col"),
        P("row", "col"),
        P("col", "row"),
    )
    out_specs = (P(("dp", "col"), "row"), P("row", ("col", "dp")), P(("col", "dp"), "row"))
    sizes = (mesh.shape["dp"], mesh.shape["row"], mesh.shape["col"])
    return jax.shard_map(
        functools.partial(shards, *sizes),
        mesh=mesh, in_specs=in_specs, out_specs=out_specs, check_vma=False,
    )
```

time: 470 us -> 134 us (0.29)
  waiting for transfers between devices: 388 us -> 0 us
  Pallas kernels: 0 us -> 115 us
  matrix products: 50.2 us -> 17.6 us
  between operations: 14.1 us -> 0.66 us
  local copies, waits for them, and re-layouts: 9.18 us -> 0.76 us
  other arithmetic: 7.37 us -> 0 us
    reduce_scatter x3 -> x0, waiting for transfers between devices: 277 us -> none  [the longest x1 135 us: shards(): lax.psum_scatter(first.astype(jnp.bfloat16), 'dp', scatter_dimension=1, t...]
    pallas_call x0 -> x1, Pallas kernels: none -> 115 us  [shards(): pl.pallas_call(functools.partial(body, n_dp, n_row, n_col), out_shape=(ja...]
    all_gather x2 -> x0, waiting for transfers between devices: 56.1 us -> none  [the longest x1 40.7 us: shards(): lax.all_gather(cotangent, 'col', axis=0, tiled=True)]
    psum x1 -> x0, waiting for transfers between devices: 53.3 us -> none  [shards(): lax.psum(lax.dot_general(cot_all, weight_out, contract, preferred_element...]
    dot_general x4 -> x2, matrix products: 50.2 us -> 17.6 us  [the longest x1 10.1 us: shards(): lax.dot_general(tok_all, gp_all, TN, preferred_element_type=f32) * factor]
    unnamed x7, local copies, waits for them, and re-layouts: 9.18 us -> 0.76 us
    convert_element_type x1 -> x0, other arithmetic: 7.37 us -> none  [shards(): lax.psum_scatter(second.astype(jnp.bfloat16), 'dp', scatter_dimension=0,...]
  transfers between devices with their start and end apart: 6 -> 0, of which waited for: 6 -> 0; matrix products, arithmetic and copies ran while one was open for 14% -> 0% of each run, Pallas kernels for 0% -> 0%
where the time goes in v1:
time: 134 us
  Pallas kernels  115 us (86%)
  matrix products  17.6 us (13%)
    pallas_call x1, Pallas kernels, shards(): pl.pallas_call(functools.partial(body, n_dp, n_row, n_col), out_shape=(ja...  115 us
    dot_general x1, matrix products, shards(): lax.dot_general(tok_all, gp_all, TN, preferred_element_type=f32) * factor  10.1 us
    dot_general x1, matrix products, shards(): lax.dot_general(hid_all, cot_all, TN, preferred_element_type=f32) * factor  7.56 us

profile of v1, /device:TPU:0, one launch (start us, length us, event | category | flops | bytes accessed | tf_op | source)
XLA Modules:
  0.0 133.8 jit_solution(7164030419813683975)
XLA Ops:
  0.6 114.8 %shard_map.76 = (bf16[4,4,64,3072]{3,2,1,0:T(8,128)(2,1)}, bf16[4,4,64,3072]{3,2,1,0:T(8,128)(2,1)}, bf16[4,256,768]{2,1,0:T(8,128)(2,1)}, bf16[4,256,768]{2,1,0:T(8,128)(2,1)}, bf16[64,3072]{1,0:T(8,128)(2,1)}) custom-call(bf16[64,3072]{1,0:T(8,128)(2,1)} %tok.1, bf16[64,3072]{1,0:T(8,128)(2,1)} %cot.1, bf16[256,3072]{1,0:T(8,128)(2,1)} %pre.1, ...), custom_call_target="tpu_custom_call" | custom-call | tf_op jit(solution)/shard_map/pallas_call | solution.py:268
  115.4 0.0 copy-start.1
  115.5 0.0 copy-start.2
  115.5 10.1 %convolution_multiply_fusion.1 = f32[3072,768]{1,0:T(8,128)} fusion(bf16[1024,3072]{1,0:T(8,128)(2,1)} %bitcast.9, bf16[1024,768]{1,0:T(8,128)(2,1)} %bitcast.11), kind=kOutput, calls=%fused_computation.1 | convolution fusion | flops 4834197504 | bytes 17301504 | tf_op jit(solution)/shard_map/dot_general | solution.py:306
  125.5 0.0 copy-done.1
  125.5 0.0 copy-done.2
  125.5 0.0 copy-start
  125.5 7.6 %convolution_multiply_fusion = f32[768,3072]{1,0:T(8,128)} fusion(bf16[1024,768]{1,0:T(8,128)(2,1)S(1)} %bitcast.10, bf16[1024,3072]{1,0:T(8,128)(2,1)S(1)} %bitcast.8), kind=kOutput, calls=%fused_computation | convolution fusion | flops 4834197504 | bytes 17301504 | tf_op jit(solution)/shard_map/dot_general | solution.py:307
  133.1 0.0 copy-done
  133.1 0.7 copy.9
Async XLA Ops:
  115.4 10.1 %copy-start.1 = (bf16[4,4,64,3072]{3,2,1,0:T(8,128)(2,1)S(1)}, bf16[4,4,64,3072]{3,2,1,0:T(8,128)(2,1)}, u32[]{:S(2)}) copy-start(bf16[4,4,64,3072]{3,2,1,0:T(8,128)(2,1)} %get-tuple-element.12) | copy-start | bytes 18874372
  115.5 10.1 %copy-start.2 = (bf16[4,256,768]{2,1,0:T(8,128)(2,1)S(1)}, bf16[4,256,768]{2,1,0:T(8,128)(2,1)}, u32[]{:S(2)}) copy-start(bf16[4,256,768]{2,1,0:T(8,128)(2,1)} %get-tuple-element.11) | copy-start | bytes 4718596
  125.5 7.6 %copy-start = (bf16[64,3072]{1,0:T(8,128)(2,1)S(1)}, bf16[64,3072]{1,0:T(8,128)(2,1)}, u32[]{:S(2)}) copy-start(bf16[64,3072]{1,0:T(8,128)(2,1)} %get-tuple-element.16) | copy-start | bytes 1179652

commit v2 on v1

v2 whole, which is shorter than its diff:
```python
import functools

import jax
import jax.numpy as jnp
from jax import lax
from jax.experimental import pallas as pl
from jax.experimental.pallas import tpu as pltpu
from jax.sharding import PartitionSpec as P

MESH = pl.DeviceIdType.MESH
NT = (((1,), (1,)), ((), ()))
TN = (((0,), (0,)), ((), ()))


def gelu_parts(a):
    half = 0.5 * (1.0 + lax.erf(a * 0.7071067811865476))
    return half * a, half + a * jnp.exp(-0.5 * a * a) * 0.3989422804014327


def tile_of(extent):
    return 256 if extent % 256 == 0 else 128


def body(
    n_dp, n_row, n_col,
    tok, cot, pre, w_in, w_out,
    tok_all, cot_all, gp_all, hid_all, grad_tok,
    win, wout, hid, slope, part, xrecv, gp, acc, cotg, term, rs,
    w_sem, l_sem, cz_s, cz_r, tz_s, tz_r, y_s, y_r, c_s, c_r,
    h_s, h_r, hf_s, hf_r, g_s, g_r, gf_s, gf_r, x_s, x_r, rs_s, rs_r,
):
    p, r, z = lax.axis_index("dp"), lax.axis_index("row"), lax.axis_index("col")
    n_y = n_dp // 2
    _, half_c, width = tok.shape
    half = n_col * half_c
    piece = half // n_row
    hidden = pre.shape[1]
    hc = hidden // n_dp
    y, c = p // 2, lax.rem(p, 2)
    partner = 2 * y + 1 - c

    def peer(m, sign=1):
        there = lax.rem(y + sign * (m // 2) + n_y, n_y)
        return 2 * there + (1 - c if m % 2 else c)

    def remote(src, dst, send, recv, where):
        return pltpu.make_async_remote_copy(
            src_ref=src, dst_ref=dst, send_sem=send, recv_sem=recv,
            device_id=where, device_id_type=MESH,
        )

    wo = pltpu.make_async_copy(w_out, wout, w_sem.at[0])
    wi = pltpu.make_async_copy(w_in, win, w_sem.at[1])
    own = pltpu.make_async_copy(cot, cotg.at[:, z], l_sem.at[0])
    wo.start()
    own.start()

    barrier = pltpu.get_barrier_semaphore()
    for axis, me, count in (("dp", p, n_dp), ("row", r, n_row), ("col", z, n_col)):
        for k in range(1, count):
            pl.semaphore_signal(
                barrier, inc=1, device_id={axis: lax.rem(me + k, count)}, device_id_type=MESH
            )
    pl.semaphore_wait(barrier, n_dp + n_row + n_col - 3)

    def block(t, blk):
        return cotg.at[t, blk] if t < 2 else tok_all.at[p, :, blk]

    def landing(t, blk):
        return cot_all.at[p, t, blk] if t < 2 else tok_all.at[p, :, blk]

    def full(t, q):
        return cot_all.at[q, t] if t < 2 else tok_all.at[q]

    def sems(t):
        return (cz_s.at[t], cz_r.at[t]) if t < 2 else (tz_s.at[0], tz_r.at[0])

    def z_copy(t, d, s):
        blk = z - s if d == 0 else z + s
        src = block(t, blk) if s else (cot.at[t] if t < 2 else tok)
        ss, rr = sems(t)
        to = z + 1 if d == 0 else z - 1
        return remote(src, block(t, blk), ss.at[d, s], rr.at[d, s + 1], {"col": to})

    def has(d, s):
        return z - s >= 0 if d == 0 else z + s < n_col

    def can_send(d, s):
        return has(d, s) & (z + 1 < n_col if d == 0 else z - 1 >= 0)

    def y_send(t, src, blk):
        for k in range(1, n_y):
            remote(
                src, landing(t, blk), y_s.at[t, k], y_r.at[t, k], {"dp": peer(2 * k)}
            ).start()

    def z_start(t):
        for d in (0, 1):
            @pl.when(can_send(d, 0))
            def _():
                z_copy(t, d, 0).start()

    def z_step(t, s):
        ss, rr = sems(t)
        for d in (0, 1):
            @pl.when(has(d, s))
            def _():
                blk = z - s if d == 0 else z + s
                remote(
                    block(t, blk), block(t, blk), ss.at[d, s], rr.at[d, s],
                    {"col": lax.rem(z + 1, n_col)},
                ).wait_recv()
                if s < n_col - 1:
                    @pl.when(can_send(d, s))
                    def _():
                        z_copy(t, d, s).start()
                y_send(t, block(t, blk), blk)

    def whole(t, at, send, recv, who):
        return remote(full(t, at), full(t, at), send, recv, {"dp": who})

    z_start(0)
    own_tok = pltpu.make_async_copy(tok, tok_all.at[p, :, z], l_sem.at[1])
    own_tok.start()
    y_send(0, cot.at[0], z)
    y_send(1, cot.at[1], z)
    y_send(2, tok, z)
    wi.start()

    def gelu_chunk(i):
        def one(j, _):
            at = pl.ds(pl.multiple_of(j * half_c, half_c), half_c)
            to = pl.ds(pl.multiple_of((j // 2) * half_c, half_c), half_c)
            a = pre[at, i * hc:(i + 1) * hc].astype(jnp.float32)
            value, sl = gelu_parts(a)
            hid[i, lax.rem(j, 2), to, :] = value.astype(jnp.bfloat16)
            slope[i, lax.rem(j, 2), to, :] = sl
            return 0
        lax.fori_loop(0, 2 * n_col, one, 0)

    done = 0
    for s in range(1, n_col):
        upto = (n_dp * s + n_col - 2) // (n_col - 1)
        for i in range(done, upto):
            gelu_chunk(i)
        done = upto
        z_step(0, s)
        if s == 1:
            z_start(1)

    rows_of = pl.ds(pl.multiple_of(r * piece, piece), piece)

    def hid_copy(m):
        q = peer(m)
        if m == 1:
            src, dst = hid.at[q], hid_all.at[p]
        else:
            src, dst = hid.at[q, :, rows_of], hid_all.at[p, :, rows_of]
        return remote(src, dst, h_s.at[m], h_r.at[m], {"dp": q})

    def hid_pass(m, k):
        ref = hid_all.at[peer(m, -1), :, rows_of]
        return remote(ref, ref, hf_s.at[m, k], hf_r.at[m, k], {"row": lax.rem(r + k, n_row)})

    def gp_copy(h, m):
        q = peer(m)
        if m == 1:
            src, dst = gp.at[q, h], gp_all.at[p, h]
        else:
            src, dst = gp.at[q, h, rows_of], gp_all.at[p, h, rows_of]
        return remote(src, dst, g_s.at[h, m], g_r.at[h, m], {"dp": q})

    def gp_pass(h, m, k):
        ref = gp_all.at[peer(m, -1), h, rows_of]
        return remote(
            ref, ref, gf_s.at[h, m, k], gf_r.at[h, m, k], {"row": lax.rem(r + k, n_row)}
        )

    for m in range(1, n_dp):
        hid_copy(m).start()
    own_hid = pltpu.make_async_copy(hid.at[p], hid_all.at[p], l_sem.at[2])
    own_hid.start()

    own.wait()
    wo.wait()
    ht = tile_of(hc)
    order = list(range(2, n_dp)) + [0, 1]

    def x_copy(h, m, k):
        q = peer(m)
        return remote(
            part.at[q, h], xrecv.at[k - 1, q, h], x_s.at[k - 1, h, m], x_r.at[k - 1, h, m],
            {"row": lax.rem(r + k, n_row)},
        )

    def part_chunk(h, m):
        q = peer(m)
        def ptile(j, _):
            off = pl.multiple_of(j * ht, ht)
            w = wout[pl.ds(pl.multiple_of(q * hc + off, ht), ht), :]
            lhs = cotg[h].reshape(half, width)
            out = lax.dot_general(lhs, w, NT, preferred_element_type=jnp.float32)
            part[q, h, :, pl.ds(off, ht)] = out.astype(jnp.bfloat16)
            return 0
        lax.fori_loop(0, hc // ht, ptile, 0)
        for k in range(1, n_row):
            x_copy(h, m, k).start()

    b_steps = 1
    for at, m in enumerate(order):
        part_chunk(0, m)
        upto = -(-(n_col - 1) * (at + 1) // n_dp)
        while b_steps <= upto:
            z_step(1, b_steps)
            if b_steps == min(2, n_col - 1):
                own_tok.wait()
                z_start(2)
            b_steps += 1
    for m in order:
        part_chunk(1, m)

    own_cot = pltpu.make_async_copy(cotg, cot_all.at[p], l_sem.at[0])
    own_cot.start()
    for t in (0, 1):
        remote(cotg.at[t], cot_all.at[p, t], c_s.at[t, 0], c_r.at[t, 0], {"dp": partner}).start()
    wi.wait()

    wt = tile_of(width)
    tok_steps = 1
    for h in (0, 1):
        for at, m in enumerate(order):
            q = peer(m)
            for k in range(1, n_row):
                x_copy(h, m, k).wait_recv()
            def one(j, _):
                rows = pl.ds(pl.multiple_of(j * half_c, half_c), half_c)
                total = part[q, h, rows, :].astype(jnp.float32)
                for k in range(1, n_row):
                    total = total + xrecv[k - 1, q, h, rows, :].astype(jnp.float32)
                gp[q, h, rows, :] = (total * slope[q, h, rows, :]).astype(jnp.bfloat16)
                return 0
            lax.fori_loop(0, n_col, one, 0)
            if m:
                gp_copy(h, m).start()
            else:
                pltpu.make_async_copy(gp.at[p, h], gp_all.at[p, h], l_sem.at[3]).start()

            def wtile(j, _):
                cols = pl.ds(pl.multiple_of(j * wt, wt), wt)
                w = win[cols, pl.ds(pl.multiple_of(q * hc, hc), hc)]
                out = lax.dot_general(gp[q, h], w, NT, preferred_element_type=jnp.float32)
                if at > 0:
                    out = acc[:, cols] + out
                if at < n_dp - 1:
                    acc[:, cols] = out
                else:
                    term[h, :, :, cols] = out.astype(jnp.bfloat16).reshape(n_col, half_c, wt)
                return 0
            lax.fori_loop(0, width // wt, wtile, 0)
            upto = -(-(n_col - 1) * (at + 1 + h * n_dp) // (n_dp + n_dp // 2))
            while tok_steps <= min(upto, n_col - 1):
                z_step(2, tok_steps)
                tok_steps += 1
        for k in range(1, n_col):
            rs_copy(remote, term, rs, rs_s, rs_r, h, k, z, n_col).start()
        if h == 0:
            for m in range(2, n_dp):
                hid_copy(m).wait_recv()
                for k in range(1, n_row):
                    hid_pass(m, k).start()
            for t in (0, 1):
                for k in range(1, n_y):
                    q = peer(2 * k, -1)
                    whole(t, q, y_s.at[t, k], y_r.at[t, k], q).wait_recv()
                    whole(t, q, c_s.at[t, k], c_r.at[t, k], partner).start()
    whole(2, p, c_s.at[2, 0], c_r.at[2, 0], partner).start()

    for h in (0, 1):
        for m in range(2, n_dp):
            gp_copy(h, m).wait_recv()
            for k in range(1, n_row):
                gp_pass(h, m, k).start()
    for k in range(1, n_y):
        q = peer(2 * k, -1)
        whole(2, q, y_s.at[2, k], y_r.at[2, k], q).wait_recv()
        whole(2, q, c_s.at[2, k], c_r.at[2, k], partner).start()

    for h in (0, 1):
        for k in range(1, n_col):
            rs_copy(remote, term, rs, rs_s, rs_r, h, k, z, n_col).wait_recv()
        total = term[h, z].astype(jnp.float32)
        for k in range(1, n_col):
            total = total + rs[h, k].astype(jnp.float32)
        grad_tok[h] = total.astype(jnp.bfloat16)

    own_hid.wait()
    own_cot.wait()
    pltpu.make_async_copy(gp.at[p], gp_all.at[p], l_sem.at[3]).wait()
    for t in (0, 1, 2):
        for d in (0, 1):
            for s in range(n_col - 1):
                @pl.when(can_send(d, s))
                def _():
                    z_copy(t, d, s).wait_send()
        for k in range(1, n_y):
            whole(t, p, y_s.at[t, k], y_r.at[t, k], peer(2 * k)).wait_send()
        for k in range(n_y):
            q = peer(2 * k, -1)
            whole(t, q, c_s.at[t, k], c_r.at[t, k], partner).wait()
    for m in range(1, n_dp):
        hid_copy(m).wait_send()
        if m == 1:
            hid_copy(m).wait_recv()
        else:
            for k in range(1, n_row):
                hid_pass(m, k).wait()
        for h in (0, 1):
            gp_copy(h, m).wait_send()
            if m == 1:
                gp_copy(h, m).wait_recv()
            else:
                for k in range(1, n_row):
                    gp_pass(h, m, k).wait()
    for h in (0, 1):
        for m in range(n_dp):
            for k in range(1, n_row):
                x_copy(h, m, k).wait_send()
        for k in range(1, n_col):
            rs_copy(remote, term, rs, rs_s, rs_r, h, k, z, n_col).wait_send()


def rs_copy(remote, term, rs, rs_s, rs_r, h, k, z, n_col):
    to = lax.rem(z + k, n_col)
    return remote(term.at[h, to], rs.at[h, k], rs_s.at[h, k], rs_r.at[h, k], {"col": to})


def shards(n_dp, n_row, n_col, tokens, cotangent, pre_act, weight_in, weight_out):
    tokc, width = tokens.shape
    rows, hidden = pre_act.shape
    hc = hidden // n_dp
    n_y = n_dp // 2
    bf, f32 = jnp.bfloat16, jnp.float32
    dma = pltpu.SemaphoreType.DMA
    anywhere = pl.BlockSpec(memory_space=pl.ANY)
    vmem = pl.BlockSpec(memory_space=pltpu.VMEM)
    half_c, half, xs = tokc // 2, rows // 2, max(n_row - 1, 1)
    tok_all, cot_all, gp_all, hid_all, grad_tokens = pl.pallas_call(
        functools.partial(body, n_dp, n_row, n_col),
        out_shape=(
            jax.ShapeDtypeStruct((n_dp, 2, n_col, half_c, width), bf),
            jax.ShapeDtypeStruct((n_dp, 2, n_col, half_c, width), bf),
            jax.ShapeDtypeStruct((n_dp, 2, half, hc), bf),
            jax.ShapeDtypeStruct((n_dp, 2, half, hc), bf),
            jax.ShapeDtypeStruct((2, half_c, width), bf),
        ),
        in_specs=[anywhere, anywhere, vmem, anywhere, anywhere],
        out_specs=(anywhere, anywhere, anywhere, anywhere, vmem),
        scratch_shapes=[
            pltpu.VMEM((width, hidden), bf),
            pltpu.VMEM((hidden, width), bf),
            pltpu.VMEM((n_dp, 2, half, hc), bf),
            pltpu.VMEM((n_dp, 2, half, hc), f32),
            pltpu.VMEM((n_dp, 2, half, hc), bf),
            pltpu.VMEM((xs, n_dp, 2, half, hc), bf),
            pltpu.VMEM((n_dp, 2, half, hc), bf),
            pltpu.VMEM((half, width), f32),
            pltpu.VMEM((2, n_col, half_c, width), bf),
            pltpu.VMEM((2, n_col, half_c, width), bf),
            pltpu.VMEM((2, n_col, half_c, width), bf),
            dma((2,)), dma((4,)),
            dma((2, 2, n_col)), dma((2, 2, n_col)), dma((1, 2, n_col)), dma((1, 2, n_col)),
            dma((3, n_y)), dma((3, n_y)), dma((3, n_y)), dma((3, n_y)),
            dma((n_dp,)), dma((n_dp,)), dma((n_dp, n_row)), dma((n_dp, n_row)),
            dma((2, n_dp)), dma((2, n_dp)), dma((2, n_dp, n_row)), dma((2, n_dp, n_row)),
            dma((xs, 2, n_dp)), dma((xs, 2, n_dp)),
            dma((2, n_col)), dma((2, n_col)),
        ],
        compiler_params=pltpu.CompilerParams(
            collective_id=0, has_side_effects=True, vmem_limit_bytes=62 * 1024 * 1024
        ),
    )(
        tokens.reshape(2, half_c, width), cotangent.reshape(2, half_c, width),
        pre_act, weight_in, weight_out,
    )
    grad_tokens = grad_tokens.reshape(tokc, width)
    total = n_dp * rows
    factor = float(total) ** (-0.5)
    tok_all, cot_all = tok_all.reshape(total, width), cot_all.reshape(total, width)
    gp_all, hid_all = gp_all.reshape(total, hc), hid_all.reshape(total, hc)
    grad_in = lax.dot_general(tok_all, gp_all, TN, preferred_element_type=f32) * factor
    grad_out = lax.dot_general(hid_all, cot_all, TN, preferred_element_type=f32) * factor
    return grad_tokens, grad_in, grad_out


def solution(mesh):
    in_specs = (
        P(("dp", "col"), "row"),
        P(("dp", "col"), "row"),
        P("dp", "col"),
        P("row", "col"),
        P("col", "row"),
    )
    out_specs = (P(("dp", "col"), "row"), P("row", ("col", "dp")), P(("col", "dp"), "row"))
    sizes = (mesh.shape["dp"], mesh.shape["row"], mesh.shape["col"])
    return jax.shard_map(
        functools.partial(shards, *sizes),
        mesh=mesh, in_specs=in_specs, out_specs=out_specs, check_vma=False,
    )
```

time: 134 us -> 119 us (0.89)
  Pallas kernels: 115 us -> 99.4 us
    pallas_call x1, Pallas kernels: 115 us -> 99.4 us  [shards(): pl.pallas_call(functools.partial(body, n_dp, n_row, n_col), out_shape=(ja...]
where the time goes in v2:
time: 119 us; the launch traced here: 118 us
  Pallas kernels  99.4 us (84%)
  matrix products  17.6 us (15%)
    pallas_call x1, Pallas kernels, shards(): pl.pallas_call(functools.partial(body, n_dp, n_row, n_col), out_shape=(ja...  99.4 us
    dot_general x1, matrix products, shards(): lax.dot_general(tok_all, gp_all, TN, preferred_element_type=f32) * factor  10.1 us
    dot_general x1, matrix products, shards(): lax.dot_general(hid_all, cot_all, TN, preferred_element_type=f32) * factor  7.56 us

profile of v2, /device:TPU:0, one launch (start us, length us, event | category | flops | bytes accessed | tf_op | source)
XLA Modules:
  0.0 118.5 jit_solution(3351521337376953929)
XLA Ops:
  0.6 99.4 %shard_map.76 = (bf16[4,2,4,32,3072]{4,3,2,1,0:T(8,128)(2,1)}, bf16[4,2,4,32,3072]{4,3,2,1,0:T(8,128)(2,1)}, bf16[4,2,128,768]{3,2,1,0:T(8,128)(2,1)}, bf16[4,2,...) custom-call(bf16[2,32,3072]{2,1,0:T(8,128)(2,1)} %bitcast.11, bf16[2,32,3072]{2,1,0:T(8,128)(2,1)} %bitcast.12, ...), custom_call_target="tpu_custom_call" | custom-call | tf_op jit(solution)/shard_map/pallas_call | solution.py:347
  100.1 0.0 copy-start.1
  100.1 0.0 copy-start.2
  100.1 10.1 %convolution_multiply_fusion.1 = f32[3072,768]{1,0:T(8,128)} fusion(bf16[1024,3072]{1,0:T(8,128)(2,1)} %bitcast.15, bf16[1024,768]{1,0:T(8,128)(2,1)} %bitcast.17), kind=kOutput, calls=%fused_computation.1 | convolution fusion | flops 4834197504 | bytes 17301504 | tf_op jit(solution)/shard_map/dot_general | solution.py:390
  110.2 0.0 copy-done.1
  110.2 0.0 copy-done.2
  110.2 0.0 copy-start
  110.2 7.6 %convolution_multiply_fusion = f32[768,3072]{1,0:T(8,128)} fusion(bf16[1024,768]{1,0:T(8,128)(2,1)S(1)} %bitcast.16, bf16[1024,3072]{1,0:T(8,128)(2,1)S(1)} %bitcast.14), kind=kOutput, calls=%fused_computation | convolution fusion | flops 4834197504 | bytes 17301504 | tf_op jit(solution)/shard_map/dot_general | solution.py:391
  117.7 0.0 copy-done
  117.7 0.7 copy.9
Async XLA Ops:
  100.1 10.1 %copy-start.1 = (bf16[4,2,4,32,3072]{4,3,2,1,0:T(8,128)(2,1)S(1)}, bf16[4,2,4,32,3072]{4,3,2,1,0:T(8,128)(2,1)}, u32[]{:S(2)}) copy-start(bf16[4,2,4,32,3072]{4,3,2,1,0:T(8,128)(2,1)} %get-tuple-element.12) | copy-start | bytes 18874372
  100.1 10.1 %copy-start.2 = (bf16[4,2,128,768]{3,2,1,0:T(8,128)(2,1)S(1)}, bf16[4,2,128,768]{3,2,1,0:T(8,128)(2,1)}, u32[]{:S(2)}) copy-start(bf16[4,2,128,768]{3,2,1,0:T(8,128)(2,1)} %get-tuple-element.11) | copy-start | bytes 4718596
  110.2 7.6 %copy-start = (bf16[2,32,3072]{2,1,0:T(8,128)(2,1)S(1)}, bf16[2,32,3072]{2,1,0:T(8,128)(2,1)}, u32[]{:S(2)}) copy-start(bf16[2,32,3072]{2,1,0:T(8,128)(2,1)} %get-tuple-element.8) | copy-start | bytes 1179652

commit v3 on v2

--- a/solution.py
+++ b/solution.py
@@ -22,10 +22,10 @@
 
 
 def body(
-    n_dp, n_row, n_col,
+    n_dp, n_row, n_col, factor,
     tok, cot, pre, w_in, w_out,
-    tok_all, cot_all, gp_all, hid_all, grad_tok,
-    win, wout, hid, slope, part, xrecv, gp, acc, cotg, term, rs,
+    tok_all, cot_all, gp_all, hid_all, grad_tok, rounded,
+    win, wout, hid, slope, part, xrecv, gp, acc, cotg, term, rs, flipped,
     w_sem, l_sem, cz_s, cz_r, tz_s, tz_r, y_s, y_r, c_s, c_r,
     h_s, h_r, hf_s, hf_r, g_s, g_r, gf_s, gf_r, x_s, x_r, rs_s, rs_r,
 ):
@@ -49,7 +49,7 @@
             device_id=where, device_id_type=MESH,
         )
 
-    wo = pltpu.make_async_copy(w_out, wout, w_sem.at[0])
+    wo = pltpu.make_async_copy(w_out, wout.at[pl.ds(0, hidden)], w_sem.at[0])
     wi = pltpu.make_async_copy(w_in, win, w_sem.at[1])
     own = pltpu.make_async_copy(cot, cotg.at[:, z], l_sem.at[0])
     wo.start()
@@ -275,6 +275,42 @@
                     whole(t, q, c_s.at[t, k], c_r.at[t, k], partner).start()
     whole(2, p, c_s.at[2, 0], c_r.at[2, 0], partner).start()
 
+    rows, total = 2 * half, n_dp * 2 * half
+    hid_copy(1).wait_recv()
+    for m in range(1, n_dp):
+        hid_copy(m).wait_send()
+        if m > 1:
+            for k in range(1, n_row):
+                hid_pass(m, k).wait_recv()
+    own_hid.wait()
+    hid_in = pltpu.make_async_copy(hid_all, hid, l_sem.at[4])
+    hid_in.start()
+    own_cot.wait()
+    for t in (0, 1):
+        for k in range(n_y):
+            q = peer(2 * k, -1) if k else p
+            whole(t, q, c_s.at[t, k], c_r.at[t, k], partner).wait_recv()
+    def bring(j, _):
+        to = pl.ds(pl.multiple_of(j * half_c, half_c), half_c)
+        src = cot_all.at[j // (2 * n_col), lax.rem(j // n_col, 2), lax.rem(j, n_col)]
+        pltpu.make_async_copy(src, wout.at[to], l_sem.at[5]).start()
+        return 0
+    lax.fori_loop(0, n_dp * 2 * n_col, bring, 0)
+    hid_in.wait()
+    for q in range(n_dp):
+        flipped[:, q * rows:(q + 1) * rows] = hid[q].reshape(rows, hc).T
+    pltpu.make_async_copy(
+        wout.at[pl.ds(0, total)], wout.at[pl.ds(0, total)], l_sem.at[5]
+    ).wait()
+    def otile(j, _):
+        cols = pl.ds(pl.multiple_of(j * wt, wt), wt)
+        out = jnp.dot(flipped[...], wout[0:total, cols], preferred_element_type=jnp.float32)
+        wout[total:total + hc, cols] = (out * factor).astype(jnp.bfloat16)
+        return 0
+    lax.fori_loop(0, width // wt, otile, 0)
+    out_copy = pltpu.make_async_copy(wout.at[pl.ds(total, hc)], rounded, l_sem.at[6])
+    out_copy.start()
+
     for h in (0, 1):
         for m in range(2, n_dp):
             gp_copy(h, m).wait_recv()
@@ -293,8 +329,7 @@
             total = total + rs[h, k].astype(jnp.float32)
         grad_tok[h] = total.astype(jnp.bfloat16)
 
-    own_hid.wait()
-    own_cot.wait()
+    out_copy.wait()
     pltpu.make_async_copy(gp.at[p], gp_all.at[p], l_sem.at[3]).wait()
     for t in (0, 1, 2):
         for d in (0, 1):
@@ -306,14 +341,14 @@
             whole(t, p, y_s.at[t, k], y_r.at[t, k], peer(2 * k)).wait_send()
         for k in range(n_y):
             q = peer(2 * k, -1)
-            whole(t, q, c_s.at[t, k], c_r.at[t, k], partner).wait()
+            copy = whole(t, q, c_s.at[t, k], c_r.at[t, k], partner)
+            copy.wait_send()
+            if t == 2:
+                copy.wait_recv()
     for m in range(1, n_dp):
-        hid_copy(m).wait_send()
-        if m == 1:
-            hid_copy(m).wait_recv()
-        else:
+        if m > 1:
             for k in range(1, n_row):
-                hid_pass(m, k).wait()
+                hid_pass(m, k).wait_send()
         for h in (0, 1):
             gp_copy(h, m).wait_send()
             if m == 1:
@@ -334,6 +369,32 @@
     return remote(term.at[h, to], rs.at[h, k], rs_s.at[h, k], rs_r.at[h, k], {"col": to})
 
 
+def finish(factor, gp, tok, rounded, grad_in, grad_out):
+    left = lax.dot_general(tok[...], gp[...], TN, preferred_element_type=jnp.float32)
+    grad_in[...] = left * factor
+    grad_out[...] = rounded[...].astype(jnp.float32)
+
+
+def weight_gradients(factor, tile, tok, gp, rounded):
+    total, width = tok.shape
+    hc = gp.shape[1]
+    f32 = jnp.float32
+    fixed = pl.BlockSpec((total, hc), lambda i: (0, 0), pipeline_mode=pl.Buffered(1))
+    moving = pl.BlockSpec((total, tile), lambda i: (0, i))
+    share = hc * tile // width
+    across = pl.BlockSpec((share, width), lambda i: (i, 0))
+    return pl.pallas_call(
+        functools.partial(finish, factor),
+        grid=(width // tile,),
+        out_shape=(
+            jax.ShapeDtypeStruct((width, hc), f32), jax.ShapeDtypeStruct((hc, width), f32)
+        ),
+        in_specs=[fixed, moving, across],
+        out_specs=(pl.BlockSpec((tile, hc), lambda i: (i, 0)), across),
+        compiler_params=pltpu.CompilerParams(vmem_limit_bytes=60 * 1024 * 1024),
+    )(gp, tok, rounded)
+
+
 def shards(n_dp, n_row, n_col, tokens, cotangent, pre_act, weight_in, weight_out):
     tokc, width = tokens.shape
     rows, hidden = pre_act.shape
@@ -343,21 +404,24 @@
     dma = pltpu.SemaphoreType.DMA
     anywhere = pl.BlockSpec(memory_space=pl.ANY)
     vmem = pl.BlockSpec(memory_space=pltpu.VMEM)
+    total = n_dp * rows
+    factor = float(total) ** (-0.5)
     half_c, half, xs = tokc // 2, rows // 2, max(n_row - 1, 1)
-    tok_all, cot_all, gp_all, hid_all, grad_tokens = pl.pallas_call(
-        functools.partial(body, n_dp, n_row, n_col),
+    tok_all, _, gp_all, _, grad_tokens, rounded = pl.pallas_call(
+        functools.partial(body, n_dp, n_row, n_col, factor),
         out_shape=(
             jax.ShapeDtypeStruct((n_dp, 2, n_col, half_c, width), bf),
             jax.ShapeDtypeStruct((n_dp, 2, n_col, half_c, width), bf),
             jax.ShapeDtypeStruct((n_dp, 2, half, hc), bf),
             jax.ShapeDtypeStruct((n_dp, 2, half, hc), bf),
             jax.ShapeDtypeStruct((2, half_c, width), bf),
+            jax.ShapeDtypeStruct((hc, width), bf),
         ),
         in_specs=[anywhere, anywhere, vmem, anywhere, anywhere],
-        out_specs=(anywhere, anywhere, anywhere, anywhere, vmem),
+        out_specs=(anywhere, anywhere, anywhere, anywhere, vmem, anywhere),
         scratch_shapes=[
             pltpu.VMEM((width, hidden), bf),
-            pltpu.VMEM((hidden, width), bf),
+            pltpu.VMEM((max(hidden, total + hc), width), bf),
             pltpu.VMEM((n_dp, 2, half, hc), bf),
             pltpu.VMEM((n_dp, 2, half, hc), f32),
             pltpu.VMEM((n_dp, 2, half, hc), bf),
@@ -367,7 +431,8 @@
             pltpu.VMEM((2, n_col, half_c, width), bf),
             pltpu.VMEM((2, n_col, half_c, width), bf),
             pltpu.VMEM((2, n_col, half_c, width), bf),
-            dma((2,)), dma((4,)),
+            pltpu.VMEM((hc, total), bf),
+            dma((2,)), dma((7,)),
             dma((2, 2, n_col)), dma((2, 2, n_col)), dma((1, 2, n_col)), dma((1, 2, n_col)),
             dma((3, n_y)), dma((3, n_y)), dma((3, n_y)), dma((3, n_y)),
             dma((n_dp,)), dma((n_dp,)), dma((n_dp, n_row)), dma((n_dp, n_row)),
@@ -383,12 +448,9 @@
         pre_act, weight_in, weight_out,
     )
     grad_tokens = grad_tokens.reshape(tokc, width)
-    total = n_dp * rows
-    factor = float(total) ** (-0.5)
-    tok_all, cot_all = tok_all.reshape(total, width), cot_all.reshape(total, width)
-    gp_all, hid_all = gp_all.reshape(total, hc), hid_all.reshape(total, hc)
-    grad_in = lax.dot_general(tok_all, gp_all, TN, preferred_element_type=f32) * factor
-    grad_out = lax.dot_general(hid_all, cot_all, TN, preferred_element_type=f32) * factor
+    tok_all, gp_all = tok_all.reshape(total, width), gp_all.reshape(total, hc)
+    tile = width // 6 if width % (6 * 128) == 0 and hc % (6 * 16) == 0 else width // 2
+    grad_in, grad_out = weight_gradients(factor, tile, tok_all, gp_all, rounded)
     return grad_tokens, grad_in, grad_out
 
 

time: 119 us -> 118 us (level)
  matrix products: 17.6 us -> 0 us
  Pallas kernels: 99.4 us -> 116 us
    dot_general x2 -> x0, matrix products: 17.6 us -> none  [the longest x1 10.1 us: shards(): lax.dot_general(tok_all, gp_all, TN, preferred_element_type=f32) * factor]
    pallas_call x1 -> x2, Pallas kernels: 99.4 us -> 116 us  [the longest x1 102 us: shards(): pl.pallas_call(functools.partial(body, n_dp, n_row, n_col, factor), out_s...]
where the time goes in v3:
time: 118 us
  Pallas kernels  116 us (98%)
    pallas_call x1, Pallas kernels, shards(): pl.pallas_call(functools.partial(body, n_dp, n_row, n_col, factor), out_s...  102 us
    pallas_call x1, Pallas kernels, weight_gradients(): pl.pallas_call(functools.partial(finish, factor), grid=(width // tile,),...  14.2 us

profile of v3, /device:TPU:0, one launch (start us, length us, event | category | flops | bytes accessed | tf_op | source)
XLA Modules:
  0.0 117.9 jit_solution(17711231943629275993)
XLA Ops:
  0.6 102.3 %shard_map.76 = (bf16[4,2,4,32,3072]{4,3,2,1,0:T(8,128)(2,1)}, bf16[4,2,4,32,3072]{4,3,2,1,0:T(8,128)(2,1)}, bf16[4,2,128,768]{3,2,1,0:T(8,128)(2,1)}, bf16[4,2,...) custom-call(bf16[2,32,3072]{2,1,0:T(8,128)(2,1)} %bitcast.7, ...), custom_call_target="tpu_custom_call" | custom-call | tf_op jit(solution)/shard_map/pallas_call | solution.py:410
  102.9 0.0 copy-start
  102.9 14.2 %shard_map.77 = (f32[3072,768]{1,0:T(8,128)}, f32[768,3072]{1,0:T(8,128)}) custom-call(bf16[1024,768]{1,0:T(8,128)(2,1)} %bitcast.6, bf16[1024,3072]{1,0:T(8,128)(2,1)} %bitcast.5, bf16[768,3072]{1,0:T(8,128)(2,1)} %get-tuple-element.12.rounded), custom_call_target="tpu_custom_call" | custom-call | tf_op jit(solution)/shard_map/pallas_call | solution.py:386
  117.1 0.0 copy-done
  117.1 0.7 copy.9
Async XLA Ops:
  102.9 14.2 %copy-start = (bf16[2,32,3072]{2,1,0:T(8,128)(2,1)S(1)}, bf16[2,32,3072]{2,1,0:T(8,128)(2,1)}, u32[]{:S(2)}) copy-start(bf16[2,32,3072]{2,1,0:T(8,128)(2,1)} %get-tuple-element.9) | copy-start | bytes 1179652
